TPU v7x, 32 devices: a whole 2x2x4 slice. The times are simulated.
32 devices in a mesh: groups: 2 (over y), expert: 2 (over core), tensor: 8 (over z, x).
Axes of the slice: x: 2, y: 2, z: 4, core: 2. Of those that a mesh axis runs over, the one named last changes fastest.
Arguments:
- tokens: bfloat16 [384, 5120], P(('groups', 'expert')), parts along dimension 0, may hold values from -6 to 6
- router_score: bfloat16 [384], P(('groups', 'expert')), parts along dimension 0, may hold values from -6 to 6
- expert_ids: int32 [384, 1], P(('groups', 'expert')), parts along dimension 0, may hold values from 0 to 1; in each aligned block of 96 rows (0 to 95, 96 to 191, ...) at most 64 rows name the same one
- gate_up: bfloat16 [2, 5120, 16384], P('expert', None, 'tensor'), may hold values from -0.078125 to 0.078125
- down: bfloat16 [2, 8192, 5120], P('expert', 'tensor'), may hold values from -0.0625 to 0.0625
- shared_gate_up: bfloat16 [5120, 8192], P(None, 'tensor'), may hold values from -0.078125 to 0.078125
- shared_down: bfloat16 [4096, 5120], P('tensor'), may hold values from -0.09375 to 0.09375
Outputs:
- mixed: bfloat16 [384, 5120], P(('groups', 'expert')), parts along dimension 0
There are 2 independent parts, one for each index of `groups`. A program takes and returns all parts, laid end to end along the dimension named above; an argument that names none is the same for every part. Nothing has to cross between parts.
Inputs may be any that keep to these rules, and one draw needn't show every extreme that they name: `expert_ids`: within the 96 rows of one index of expert no expert is chosen by more than 64 rows, a bound that some block reaches.
All inputs are finite; a program needn't handle non-finite values.
Results may differ from a plain program's by a relative error of at most 0.0052.
Values may be sent and summed in bfloat16 or wider, within the bound.
A program may use at most 128 MiB of HBM per device.

v0:
```python
import jax
import jax.numpy as jnp
from jax import lax
from jax.sharding import PartitionSpec as P

CAP = 64


def joined_hidden(inputs, weights):
    both = jnp.dot(inputs, weights, preferred_element_type=jnp.float32)
    half_width = weights.shape[1] // 2
    return (jax.nn.silu(both[:, :half_width]) * both[:, half_width:]).astype(jnp.bfloat16)


def on_device(tokens, router_score, expert_ids, gate_up, down, shared_gate_up, shared_down):
    model_width = tokens.shape[1]
    groups_exp = lax.axis_size("expert")
    slots = groups_exp * CAP
    chosen = expert_ids[:, 0]
    member = (chosen[:, None] == jnp.arange(groups_exp, dtype=jnp.int32)[None, :]).astype(jnp.int32)
    before = jnp.cumsum(member, axis=0) - member
    target = chosen * CAP + jnp.sum(before * member, axis=1)
    placing = (jnp.arange(slots, dtype=jnp.int32)[:, None] == target[None, :]).astype(jnp.bfloat16)
    packed = jnp.dot(placing, tokens, preferred_element_type=jnp.float32).astype(jnp.bfloat16)
    packed = packed.reshape(groups_exp, CAP, model_width)
    packed_score = jnp.dot(placing, router_score[:, None], preferred_element_type=jnp.float32)
    packed_score = packed_score.astype(jnp.bfloat16).reshape(groups_exp, CAP)
    arrived, arrived_score = (
        lax.all_to_all(packed, "expert", split_axis=0, concat_axis=0, tiled=True),
        lax.all_to_all(packed_score, "expert", split_axis=0, concat_axis=0, tiled=True),
    )
    inputs = arrived.reshape(slots, model_width)
    factor = jax.nn.sigmoid(arrived_score.reshape(slots, 1).astype(jnp.float32))
    scaled = (inputs.astype(jnp.float32) * factor).astype(jnp.bfloat16)
    routed_hidden = joined_hidden(scaled, gate_up[0])
    shared_hidden = joined_hidden(inputs, shared_gate_up)
    returned = None
    result = None
    routed_part = jnp.dot(routed_hidden, down[0], preferred_element_type=jnp.float32)
    result = lax.psum(
        routed_part + jnp.dot(shared_hidden, shared_down, preferred_element_type=jnp.float32),
        "tensor",
    ).astype(jnp.bfloat16)
    returned = lax.all_to_all(
        result.reshape(groups_exp, CAP, model_width),
        "expert",
        split_axis=0,
        concat_axis=0,
        tiled=True,
    )
    mixed = jnp.dot(
        placing.T, returned.reshape(slots, model_width), preferred_element_type=jnp.float32
    )
    return mixed.astype(jnp.bfloat16)


def solution(mesh):
    placed = (
        P(("groups", "expert"), None),
        P(("groups", "expert")),
        P(("groups", "expert"), None),
        P("expert", None, "tensor"),
        P("expert", "tensor", None),
        P(None, "tensor"),
        P("tensor", None),
    )
    return jax.shard_map(
        on_device,
        mesh=mesh,
        in_specs=placed,
        out_specs=P(("groups", "expert"), None),
        check_vma=False,
    )
```

profile of v0, /device:TPU:0, one launch (start us, length us, event | category | flops | bytes accessed | tf_op | source)
XLA Modules:
  0.0 150.2 jit_solution(5042480018702754999)
XLA Ops:
  0.0 0.0 copy-start
  0.0 0.8 fusion.11
  0.8 0.1 reduce_window_sum.11
  1.0 0.8 select_reduce_fusion
  1.8 0.7 multiply_add_fusion
  2.5 0.0 copy-done
  2.5 1.6 %convolution_convert_fusion = bf16[128,5120]{1,0:T(8,128)(2,1)} fusion(bf16[96,5120]{1,0:T(8,128)(2,1)S(1)} %copy-done, s32[96]{0:T(128)S(1)} %multiply_add_fusion), kind=kOutput, calls=%fused_computation.5 | convolution fusion | flops 126496768 | bytes 2294144 | tf_op jit(solution)/shard_map/dot_general | solution.py:24
  4.0 3.6 %all-to-all-start = ((bf16[2,64,5120]{2,1,0:T(8,128)(2,1)}), bf16[2,64,5120]{2,1,0:T(8,128)(2,1)S(1)}, u32[]{:S(2)}, u32[]{:S(2)}) async-start(bf16[2,64,5120]{2,1,0:T(8,128)(2,1)} %bitcast.33), calls=%async_computation | async-start | bytes 2621440 | tf_op jit(solution)/shard_map/all_to_all | solution.py:29
  7.7 0.0 copy-done.1
  7.7 0.1 fusion.4
  7.8 0.7 all_to_all.16
  8.5 1.5 all-to-all-done
  10.0 3.2 %all-to-all-start.1 = ((bf16[2,1,64]{2,1,0:T(2,128)(2,1)}), bf16[2,1,64]{2,1,0:T(2,128)(2,1)S(1)}, u32[]{:S(2)}, u32[]{:S(2)}) async-start(bf16[2,1,64]{2,1,0:T(2,128)(2,1)} %all_to_all.16), calls=%async_computation.1 | async-start | bytes 2048 | tf_op jit(solution)/shard_map/all_to_all | solution.py:30
  13.2 5.5 %fusion.18 = f32[128,1024]{1,0:T(8,128)S(1)} fusion(bf16[128,5120]{1,0:T(8,128)(2,1)S(1)} %bitcast.27, bf16[5120,1024]{1,0:T(8,128)(2,1)} %param.12), kind=kOutput, calls=%fused_computation.28 | convolution fusion | flops 1342177280 | bytes 12320768 | tf_op jit(solution)/shard_map/dot_general | solution.py:10
  18.7 0.0 all-to-all-done.1
  18.7 0.0 slice-start
  18.7 0.0 slice-start.3
  18.7 0.3 multiply_convert_fusion
  19.0 0.0 slice-start.1
  19.1 0.0 slice-start.2
  19.1 0.0 slice-start.4
  19.1 8.7 %fusion = f32[128,2048]{1,0:T(8,128)S(1)} fusion(bf16[128,5120]{1,0:T(8,128)(2,1)S(1)} %bitcast.32, bf16[1,5120,2048]{2,1,0:T(8,128)(2,1)} %param.10), kind=kOutput, calls=%fused_computation | convolution fusion | flops 2684354560 | bytes 23330816 | tf_op jit(solution)/shard_map/dot_general | solution.py:10
  27.8 0.0 slice-done
  27.8 1.6 %slice-done.1 = s8[4194304]{0:T(1024)(128)(4,1)S(1)} async-done(((s8[10485760]{0:T(1024)(128)(4,1)}), s8[4194304]{0:T(1024)(128)(4,1)S(1)}, s32[]{:S(2)}) %slice-start.1) | async-done | bytes 4194328
  29.4 0.6 slice-done.2
  30.0 1.6 %fusion.2 = f32[128,5120]{1,0:T(8,128)S(1)} fusion(bf16[1,1024,5120]{2,1,0:T(8,128)(2,1)S(1)} %bitcast.29, f32[128,2048]{1,0:T(8,128)S(1)} %fusion), kind=kOutput, calls=%fused_computation.2 | convolution fusion | flops 1342963712 | bytes 14155776 | tf_op jit(solution)/shard_map/dot_general | solution.py:39
  31.6 0.0 slice-done.3
  31.6 0.0 slice-done.4
  31.6 2.4 %convolution_add_fusion = f32[128,5120]{1,0:T(8,128)} fusion(f32[128,5120]{1,0:T(8,128)S(1)} %fusion.2, bf16[512,5120]{1,0:T(8,128)(2,1)S(1)} %bitcast.31, f32[128,1024]{1,0:T(8,128)S(1)} %fusion.18), kind=kOutput, calls=%fused_computation.4 | convolution fusion | flops 672137216 | bytes 11010048 | tf_op jit(solution)/shard_map/dot_general | solution.py:41
  34.0 110.0 %all-reduce.1 = bf16[128,5120]{1,0:T(8,128)(2,1)S(1)} all-reduce(f32[128,5120]{1,0:T(8,128)} %convolution_add_fusion), channel_id=1, replica_groups=mesh['groups'=2,'expert'=2,'tensor'=8] {'tensor'}, use_global_device_ids=true, to_apply=%region_2.3 | all-reduce | flops 655360 | bytes 3932160 | tf_op jit(solution)/shard_map/psum | solution.py:40
  144.0 4.8 %all_to_all.20 = bf16[2,64,5120]{2,1,0:T(8,128)(2,1)S(1)} all-to-all(bf16[2,64,5120]{2,1,0:T(8,128)(2,1)S(1)} %bitcast.35), channel_id=1, replica_groups=mesh['groups'=2,'expert'=2,'tensor'=8] {'expert'}, dimensions={0} | all-to-all | bytes 2621440 | tf_op jit(solution)/shard_map/all_to_all | solution.py:44
  148.8 1.4 convolution_convert_fusion.1
  (4 shorter events, 0.0 us)
Async XLA Ops:
  0.0 2.5 %copy-start = (bf16[96,5120]{1,0:T(8,128)(2,1)S(1)}, bf16[96,5120]{1,0:T(8,128)(2,1)}, u32[]{:S(2)}) copy-start(bf16[96,5120]{1,0:T(8,128)(2,1)} %param.7) | copy-start | bytes 2949124
  0.0 7.7 %copy-start.1 = (bf16[96]{0:T(256)(128)(2,1)S(1)}, bf16[96]{0:T(256)(128)(2,1)}, u32[]{:S(2)}) copy-start(bf16[96]{0:T(256)(128)(2,1)} %param.8) | copy-start | bytes 580
  4.0 5.9 %all-to-all-start = ((bf16[2,64,5120]{2,1,0:T(8,128)(2,1)}), bf16[2,64,5120]{2,1,0:T(8,128)(2,1)S(1)}, u32[]{:S(2)}, u32[]{:S(2)}) async-start(bf16[2,64,5120]{2,1,0:T(8,128)(2,1)} %bitcast.33), calls=%async_computation | async-start | bytes 2621440 | tf_op jit(solution)/shard_map/all_to_all | solution.py:29
  10.0 8.7 %all-to-all-start.1 = ((bf16[2,1,64]{2,1,0:T(2,128)(2,1)}), bf16[2,1,64]{2,1,0:T(2,128)(2,1)S(1)}, u32[]{:S(2)}, u32[]{:S(2)}) async-start(bf16[2,1,64]{2,1,0:T(2,128)(2,1)} %all_to_all.16), calls=%async_computation.1 | async-start | bytes 2048 | tf_op jit(solution)/shard_map/all_to_all | solution.py:30
  18.7 9.1 %slice-start = ((s8[10485760]{0:T(1024)(128)(4,1)}), s8[4194304]{0:T(1024)(128)(4,1)S(1)}, s32[]{:S(2)}) async-start(s8[10485760]{0:T(1024)(128)(4,1)} %bitcast.28), calls=%async_computation.3 | async-start | bytes 8388608
  18.7 12.9 %slice-start.3 = ((s8[5242880]{0:T(1024)(128)(4,1)}), s8[4194304]{0:T(1024)(128)(4,1)S(1)}, s32[]{:S(2)}) async-start(s8[5242880]{0:T(1024)(128)(4,1)} %bitcast.30), calls=%async_computation.6 | async-start | bytes 8388608
  19.0 10.4 %slice-start.1 = ((s8[10485760]{0:T(1024)(128)(4,1)}), s8[4194304]{0:T(1024)(128)(4,1)S(1)}, s32[]{:S(2)}) async-start(s8[10485760]{0:T(1024)(128)(4,1)} %bitcast.28), calls=%async_computation.4 | async-start | bytes 8388608
  19.1 11.0 %slice-start.2 = ((s8[10485760]{0:T(1024)(128)(4,1)}), s8[2097152]{0:T(1024)(128)(4,1)S(1)}, s32[]{:S(2)}) async-start(s8[10485760]{0:T(1024)(128)(4,1)} %bitcast.28), calls=%async_computation.5 | async-start | bytes 4194304
  19.1 12.5 %slice-start.4 = ((s8[5242880]{0:T(1024)(128)(4,1)}), s8[1048576]{0:T(1024)(128)(4,1)S(1)}, s32[]{:S(2)}) async-start(s8[5242880]{0:T(1024)(128)(4,1)} %bitcast.30), calls=%async_computation.7 | async-start | bytes 2097152
where the time goes:
time: 151 us; the launch traced here: 150 us
  blocking collectives  115 us (76%)
  matrix products  21.3 us (14%)
  starting transfers between devices  6.82 us (5%)
  local copies, waits for them, and re-layouts  2.93 us (2%)
  other arithmetic  2.77 us (2%)
    psum x1, blocking collectives, on_device(): lax.psum(routed_part + jnp.dot(shared_hidden, shared_down, preferred_elem...  110 us
    dot_general x2, matrix products, joined_hidden(): both = jnp.dot(inputs, weights, preferred_element_type=jnp.float32)  14.2 us
    all_to_all x1, blocking collectives, on_device(): lax.all_to_all(result.reshape(groups_exp, CAP, model_width), 'expert', sp...  4.79 us
    all_to_all x1, starting transfers between devices, on_device(): lax.all_to_all(packed, 'expert', split_axis=0, concat_axis=0, tiled=True)  3.63 us
    all_to_all x1, starting transfers between devices, on_device(): lax.all_to_all(packed_score, 'expert', split_axis=0, concat_axis=0, tiled...  3.2 us
  transfers between devices with their start and end apart: 2, of which 1 were waited for; matrix products, arithmetic and copies ran while one was open for 4% of the time, Pallas kernels for 0%

commit v1 on v0

--- a/solution.py
+++ b/solution.py
@@ -1,9 +1,273 @@
 import jax
 import jax.numpy as jnp
 from jax import lax
+from jax.experimental import pallas as pl
+from jax.experimental.pallas import tpu as pltpu
 from jax.sharding import PartitionSpec as P
 
 CAP = 64
+MESH = pl.DeviceIdType.MESH
+UNITS = 256
+WIDE = 1024
+NZ, NX = 4, 2
+
+
+def fused_kernel(
+    tok_ref, score_ref, ids_ref, gu_ref, down_ref, sgu_ref, sdown_ref, out_ref,
+    w1, w2, lhs, aux, hidden, part, core_out, core_in, xsum, x_out, x_in, zsum, z_out, z_in,
+    w1_sem, w2_sem, tok_sem, tok_send, tok_recv,
+    core_send, core_recv, x_send, x_recv, z_send, z_recv, gz_send, gz_recv, gx_send, gx_recv,
+):
+    rows, width = tok_ref.shape
+    half = rows // NX
+    routed = gu_ref.shape[1] // 2
+    shared = sgu_ref.shape[1] // 2
+    own_shared = shared // 2
+    first_steps = w1.shape[0]
+    chunks = w2.shape[0]
+    piece = WIDE // NZ
+    me = lax.axis_index("expert")
+    tensor = lax.axis_index("tensor")
+    z, x = tensor // NX, lax.rem(tensor, NX)
+    core = {"expert": 1 - me}
+    xpeer = {"tensor": z * NX + 1 - x}
+    zpeer = [{"tensor": lax.rem(z + d, NZ) * NX + x} for d in range(1, NZ)]
+
+    def w1_copies(j):
+        if j == 0:
+            at = pl.multiple_of(me * own_shared, own_shared)
+            pair = (sgu_ref.at[:, pl.ds(at, UNITS)], sgu_ref.at[:, pl.ds(shared + at, UNITS)])
+        else:
+            at = (j - 1) * UNITS
+            pair = (gu_ref.at[:, pl.ds(at, UNITS)], gu_ref.at[:, pl.ds(routed + at, UNITS)])
+        return [
+            pltpu.make_async_copy(src, w1.at[j, :, pl.ds(i * UNITS, UNITS)], w1_sem.at[j, i])
+            for i, src in enumerate(pair)
+        ]
+
+    def w2_copies(c):
+        cols = pl.ds(c * WIDE, WIDE)
+        at = pl.multiple_of(me * own_shared, own_shared)
+        return [
+            pltpu.make_async_copy(down_ref.at[:, cols], w2.at[c, pl.ds(0, routed)], w2_sem.at[c, 0]),
+            pltpu.make_async_copy(
+                sdown_ref.at[pl.ds(at, own_shared), cols],
+                w2.at[c, pl.ds(routed, own_shared)],
+                w2_sem.at[c, 1],
+            ),
+        ]
+
+    own_tok = pltpu.make_async_copy(tok_ref, lhs.at[0, pl.ds(0, rows)], tok_sem.at[0])
+    own_tok.start()
+    for j in range(first_steps):
+        for copy in w1_copies(j):
+            copy.start()
+    for c in range(chunks):
+        for copy in w2_copies(c):
+            copy.start()
+
+    score = score_ref[...].astype(jnp.float32)
+    diagonal = lax.broadcasted_iota(jnp.int32, (rows, rows), 0) == lax.broadcasted_iota(
+        jnp.int32, (rows, rows), 1
+    )
+    score = jnp.sum(jnp.where(diagonal, score, 0.0), axis=1, keepdims=True)
+    factor = 1.0 / (1.0 + jnp.exp(-score))
+    lane = lax.broadcasted_iota(jnp.int32, (rows, 128), 1)
+    aux[0] = jnp.where(lane == 0, factor, ids_ref[...].astype(jnp.float32))
+
+    barrier = pltpu.get_barrier_semaphore()
+    for peer in [core, xpeer] + zpeer:
+        pl.semaphore_signal(barrier, inc=1, device_id=peer, device_id_type=MESH)
+    pl.semaphore_wait(barrier, 1 + 1 + NZ - 1)
+
+    def remote(src, dst, send, recv, peer):
+        return pltpu.make_async_remote_copy(
+            src_ref=src, dst_ref=dst, send_sem=send, recv_sem=recv, device_id=peer,
+            device_id_type=MESH,
+        )
+
+    tok_copy = remote(tok_ref, lhs.at[0, pl.ds(rows, rows)], tok_send.at[0], tok_recv.at[0], core)
+    aux_copy = remote(aux.at[0], aux.at[1], tok_send.at[1], tok_recv.at[1], core)
+    aux_copy.start()
+    tok_copy.start()
+
+    def scale(which):
+        col = aux[which, :, 0:1]
+
+        def body(i, carry):
+            cols = pl.ds(pl.multiple_of(i * 512, 512), 512)
+            at = pl.ds(which * rows, rows)
+            lhs[1, at, cols] = (lhs[0, at, cols].astype(jnp.float32) * col).astype(jnp.bfloat16)
+            return carry
+
+        lax.fori_loop(0, width // 512, body, 0)
+
+    own_tok.wait()
+    scale(0)
+    aux_copy.wait()
+    tok_copy.wait()
+    scale(1)
+
+    mine = jnp.concatenate([aux[0, :, 1:2], aux[1, :, 1:2]], axis=0) == me.astype(jnp.float32)
+
+    def first(j, carry):
+        for i in range(2):
+            block = w1.at[j, :, pl.ds(i * UNITS, UNITS)]
+            pltpu.make_async_copy(block, block, w1_sem.at[j, i]).wait()
+        both = jnp.dot(lhs[jnp.minimum(j, 1)], w1[j], preferred_element_type=jnp.float32)
+        gate, up = both[:, :UNITS], both[:, UNITS:]
+        unit = gate / (1.0 + jnp.exp(-gate)) * up
+        unit = jnp.where(jnp.logical_or(mine, j == 0), unit, 0.0)
+        hidden[j] = unit.astype(jnp.bfloat16)
+        return carry
+
+    lax.fori_loop(0, first_steps, first, 0)
+
+    def core_copy(c):
+        return remote(core_out.at[c], core_in.at[c], core_send.at[c], core_recv.at[c], core)
+
+    def x_copy(c):
+        return remote(x_out.at[c], x_in.at[c], x_send.at[c], x_recv.at[c], xpeer)
+
+    def z_copy(c, d):
+        there = lax.rem(z + d, NZ)
+        return remote(
+            z_out.at[c, there], z_in.at[c, d - 1], z_send.at[c, d - 1], z_recv.at[c, d - 1],
+            zpeer[d - 1],
+        )
+
+    def columns(c, source):
+        return pl.ds(pl.multiple_of(c * WIDE + source * piece, piece), piece)
+
+    def gz_copy(c, d, source):
+        block = out_ref.at[x, :, columns(c, source)]
+        return remote(block, block, gz_send.at[c, d - 1], gz_recv.at[c, d - 1], zpeer[d - 1])
+
+    def gx_copy(c, side):
+        block = out_ref.at[side, :, pl.ds(pl.multiple_of(c * WIDE, WIDE), WIDE)]
+        return remote(block, block, gx_send.at[c], gx_recv.at[c], xpeer)
+
+    def second(c):
+        for i, (at, size) in enumerate(((0, routed), (routed, own_shared))):
+            block = w2.at[c, pl.ds(at, size)]
+            pltpu.make_async_copy(block, block, w2_sem.at[c, i]).wait()
+        for n in range(WIDE // 512):
+            cols = pl.ds(n * 512, 512)
+            total = None
+            for j in range(first_steps):
+                at = routed if j == 0 else (j - 1) * UNITS
+                term = jnp.dot(
+                    hidden[j], w2[c, pl.ds(at, UNITS), cols], preferred_element_type=jnp.float32
+                )
+                total = term if total is None else total + term
+            part[c, :, cols] = total[:rows]
+            core_out[c, :, cols] = total[rows:].astype(jnp.bfloat16)
+        core_copy(c).start()
+
+    def join_cores(c):
+        core_copy(c).wait_recv()
+        total = part[c] + core_in[c].astype(jnp.float32)
+        xsum[0] = total[:half]
+        xsum[1] = total[half:]
+        zsum[c] = xsum[x]
+        x_out[c] = xsum[1 - x].astype(jnp.bfloat16)
+        x_copy(c).start()
+
+    def join_x(c):
+        x_copy(c).wait_recv()
+        total = zsum[c] + x_in[c].astype(jnp.float32)
+        zsum[c] = total
+        for k in range(NZ):
+            z_out[c, k] = total[:, k * piece:(k + 1) * piece].astype(jnp.bfloat16)
+        for d in (2, 1, 3):
+            z_copy(c, d).start()
+
+    def join_z(c):
+        total = zsum[c, :, pl.ds(pl.multiple_of(z * piece, piece), piece)]
+        for d in range(1, NZ):
+            z_copy(c, d).wait_recv()
+            total = total + z_in[c, d - 1].astype(jnp.float32)
+        out_ref[x, :, columns(c, z)] = total.astype(jnp.bfloat16)
+        for d in (2, 1, 3):
+            gz_copy(c, d, z).start()
+
+    def pass_x(c):
+        for d in range(1, NZ):
+            gz_copy(c, d, lax.rem(z + NZ - d, NZ)).wait_recv()
+        gx_copy(c, x).start()
+
+    stages = ((0, second), (1, join_cores), (3, join_x), (4, join_z), (5, pass_x))
+
+    def step(s, carry):
+        for lag, stage in stages:
+            c = s - lag
+
+            @pl.when(jnp.logical_and(c >= 0, c < chunks))
+            def _(stage=stage, c=c):
+                stage(c)
+
+        return carry
+
+    lax.fori_loop(0, chunks + stages[-1][0], step, 0)
+
+    def finish(c, carry):
+        gx_copy(c, 1 - x).wait_recv()
+        gx_copy(c, x).wait_send()
+        core_copy(c).wait_send()
+        x_copy(c).wait_send()
+        for d in range(1, NZ):
+            z_copy(c, d).wait_send()
+            gz_copy(c, d, z).wait_send()
+        return carry
+
+    lax.fori_loop(0, chunks, finish, 0)
+
+
+def fused_device(tokens, router_score, expert_ids, gate_up, down, shared_gate_up, shared_down):
+    rows, width = tokens.shape
+    half = rows // NX
+    routed, own_shared = down.shape[1], shared_down.shape[0] // 2
+    units = routed + own_shared
+    steps, chunks = units // UNITS, width // WIDE
+    bf16, f32 = jnp.bfloat16, jnp.float32
+    any_space = pl.BlockSpec(memory_space=pl.ANY)
+    vmem = pl.BlockSpec(memory_space=pltpu.VMEM)
+    dma = pltpu.SemaphoreType.DMA
+    out = pl.pallas_call(
+        fused_kernel,
+        out_shape=jax.ShapeDtypeStruct((NX, half, width), bf16),
+        in_specs=[any_space, vmem, vmem] + [any_space] * 4,
+        out_specs=vmem,
+        scratch_shapes=[
+            pltpu.VMEM((steps, width, 2 * UNITS), bf16),
+            pltpu.VMEM((chunks, units, WIDE), bf16),
+            pltpu.VMEM((2, 2 * rows, width), bf16),
+            pltpu.VMEM((2, rows, 128), f32),
+            pltpu.VMEM((steps, 2 * rows, UNITS), bf16),
+            pltpu.VMEM((chunks, rows, WIDE), f32),
+            pltpu.VMEM((chunks, rows, WIDE), bf16),
+            pltpu.VMEM((chunks, rows, WIDE), bf16),
+            pltpu.VMEM((NX, half, WIDE), f32),
+            pltpu.VMEM((chunks, half, WIDE), bf16),
+            pltpu.VMEM((chunks, half, WIDE), bf16),
+            pltpu.VMEM((chunks, half, WIDE), f32),
+            pltpu.VMEM((chunks, NZ, half, WIDE // NZ), bf16),
+            pltpu.VMEM((chunks, NZ - 1, half, WIDE // NZ), bf16),
+            dma((steps, 2)), dma((chunks, 2)), dma((1,)), dma((2,)), dma((2,)),
+            dma((chunks,)), dma((chunks,)), dma((chunks,)), dma((chunks,)),
+            dma((chunks, NZ - 1)), dma((chunks, NZ - 1)),
+            dma((chunks, NZ - 1)), dma((chunks, NZ - 1)),
+            dma((chunks,)), dma((chunks,)),
+        ],
+        compiler_params=pltpu.CompilerParams(
+            collective_id=0, has_side_effects=True, vmem_limit_bytes=62 * 1024 * 1024
+        ),
+        name="fused_experts",
+    )(
+        tokens, router_score.reshape(1, rows), expert_ids, gate_up[0], down[0],
+        shared_gate_up, shared_down,
+    )
+    return out.reshape(rows, width)
 
 
 def joined_hidden(inputs, weights):
@@ -54,6 +318,10 @@
     return mixed.astype(jnp.bfloat16)
 
 
+def fits_kernel(mesh):
+    return dict(mesh.shape) == {"groups": 2, "expert": 2, "tensor": NZ * NX}
+
+
 def solution(mesh):
     placed = (
         P(("groups", "expert"), None),
@@ -65,7 +333,7 @@
         P("tensor", None),
     )
     return jax.shard_map(
-        on_device,
+        fused_device if fits_kernel(mesh) else on_device,
         mesh=mesh,
         in_specs=placed,
         out_specs=P(("groups", "expert"), None),

time: 151 us -> 63.4 us (0.42)
  blocking collectives: 115 us -> 0 us
  Pallas kernels: 0 us -> 59.6 us
  matrix products: 21.3 us -> 0 us
  starting transfers between devices: 6.82 us -> 0 us
  other arithmetic: 2.77 us -> 0 us
    psum x1 -> x0, blocking collectives: 110 us -> none  [on_device(): lax.psum(routed_part + jnp.dot(shared_hidden, shared_down, preferred_elem...]
    pallas_call x0 -> x1, Pallas kernels: none -> 59.6 us  [fused_device(): pl.pallas_call(fused_kernel, out_shape=jax.ShapeDtypeStruct((NX, half, wi...]
    dot_general x7 -> x0, matrix products: 21.3 us -> none  [the longest x2 14.2 us: joined_hidden(): both = jnp.dot(inputs, weights, preferred_element_type=jnp.float32)]
    all_to_all x2 -> x0, starting transfers between devices: 6.82 us -> none  [the longest x1 3.63 us: on_device(): lax.all_to_all(packed, 'expert', split_axis=0, concat_axis=0, tiled=True)]
    all_to_all x1 -> x0, blocking collectives: 4.79 us -> none  [on_device(): lax.all_to_all(result.reshape(groups_exp, CAP, model_width), 'expert', sp...]
    unnamed x14 -> x2, local copies, waits for them, and re-layouts: 2.26 us -> 3.58 us
  transfers between devices with their start and end apart: 2 -> 0, of which waited for: 1 -> 0; matrix products, arithmetic and copies ran while one was open for 4% -> 0% of each run, Pallas kernels for 0% -> 0%
where the time goes in v1:
time: 63.4 us; the launch traced here: 63.2 us
  Pallas kernels  59.6 us (94%)
  local copies, waits for them, and re-layouts  3.58 us (6%)
    pallas_call x1, Pallas kernels, fused_device(): pl.pallas_call(fused_kernel, out_shape=jax.ShapeDtypeStruct((NX, half, wi...  59.6 us
    unnamed x2, local copies, waits for them, and re-layouts  3.58 us

profile of v1, /device:TPU:0, one launch (start us, length us, event | category | flops | bytes accessed | tf_op | source)
XLA Modules:
  0.0 63.2 jit_solution(7364959344650331957)
XLA Ops:
  0.0 1.4 %copy.8.ids_ref = s32[96,1]{1,0:T(8,128)} copy(s32[96,1]{0,1:T(1,128)} %param.9) | data formatting | bytes 768 | tf_op args[2]
  1.4 59.6 %fused_experts.1 = bf16[2,48,5120]{2,1,0:T(8,128)(2,1)} custom-call(bf16[96,5120]{1,0:T(8,128)(2,1)} %tok_ref.1, bf16[1,96]{1,0:T(2,128)(2,1)} %bitcast.7, s32[96,1]{1,0:T(8,128)} %copy.8.ids_ref, bf16[5120,2048]{1,0:T(8,128)(2,1)} %bitcast.4, bf16[1024,5120]{1,0:T(8,128)(2,1)} %bitcast.5, bf16[5120,1024]{1,0:T(8,128)(2,1)} %sgu_ref.1, ...), custom_call_target="tpu_custom_call" | custom-call | tf_op jit(solution)/shard_map/fused_experts/pallas_call | solution.py:236
  61.0 2.2 %copy.10 = bf16[96,5120]{1,0:T(8,128)(2,1)} copy(bf16[96,5120]{1,0:T(8,128)(2,1)} %bitcast.6) | data formatting | bytes 1966080

commit v2 on v1

--- a/solution.py
+++ b/solution.py
@@ -8,7 +8,7 @@
 CAP = 64
 MESH = pl.DeviceIdType.MESH
 UNITS = 256
-WIDE = 1024
+WIDE = 512
 NZ, NX = 4, 2
 
 
@@ -16,7 +16,7 @@
     tok_ref, score_ref, ids_ref, gu_ref, down_ref, sgu_ref, sdown_ref, out_ref,
     w1, w2, lhs, aux, hidden, part, core_out, core_in, xsum, x_out, x_in, zsum, z_out, z_in,
     w1_sem, w2_sem, tok_sem, tok_send, tok_recv,
-    core_send, core_recv, x_send, x_recv, z_send, z_recv, gz_send, gz_recv, gx_send, gx_recv,
+    core_send, core_recv, x_send, x_recv, z_send, z_recv, m_send, m_recv, g_send, g_recv, gx_send, gx_recv,
 ):
     rows, width = tok_ref.shape
     half = rows // NX
@@ -25,13 +25,14 @@
     own_shared = shared // 2
     first_steps = w1.shape[0]
     chunks = w2.shape[0]
-    piece = WIDE // NZ
     me = lax.axis_index("expert")
     tensor = lax.axis_index("tensor")
     z, x = tensor // NX, lax.rem(tensor, NX)
     core = {"expert": 1 - me}
     xpeer = {"tensor": z * NX + 1 - x}
-    zpeer = [{"tensor": lax.rem(z + d, NZ) * NX + x} for d in range(1, NZ)]
+    inner = jnp.logical_or(z == 1, z == 2)
+    zpeer = {"tensor": (z + 1 - 2 * lax.rem(z, 2)) * NX + x}
+    mpeer = {"tensor": (NZ - 1 - z) * NX + x}
 
     def w1_copies(j):
         if j == 0:
@@ -62,23 +63,22 @@
     for j in range(first_steps):
         for copy in w1_copies(j):
             copy.start()
-    for c in range(chunks):
-        for copy in w2_copies(c):
-            copy.start()
 
     score = score_ref[...].astype(jnp.float32)
     diagonal = lax.broadcasted_iota(jnp.int32, (rows, rows), 0) == lax.broadcasted_iota(
         jnp.int32, (rows, rows), 1
     )
     score = jnp.sum(jnp.where(diagonal, score, 0.0), axis=1, keepdims=True)
+    ids = jnp.where(diagonal, ids_ref[...].astype(jnp.float32), 0.0)
+    ids = jnp.sum(ids, axis=1, keepdims=True)
     factor = 1.0 / (1.0 + jnp.exp(-score))
     lane = lax.broadcasted_iota(jnp.int32, (rows, 128), 1)
-    aux[0] = jnp.where(lane == 0, factor, ids_ref[...].astype(jnp.float32))
+    aux[0] = jnp.where(lane == 0, factor, ids)
 
     barrier = pltpu.get_barrier_semaphore()
-    for peer in [core, xpeer] + zpeer:
+    for peer in (core, xpeer, zpeer, mpeer):
         pl.semaphore_signal(barrier, inc=1, device_id=peer, device_id_type=MESH)
-    pl.semaphore_wait(barrier, 1 + 1 + NZ - 1)
+    pl.semaphore_wait(barrier, 4)
 
     def remote(src, dst, send, recv, peer):
         return pltpu.make_async_remote_copy(
@@ -104,6 +104,9 @@
 
     own_tok.wait()
     scale(0)
+    for c in range(chunks):
+        for copy in w2_copies(c):
+            copy.start()
     aux_copy.wait()
     tok_copy.wait()
     scale(1)
@@ -129,22 +132,21 @@
     def x_copy(c):
         return remote(x_out.at[c], x_in.at[c], x_send.at[c], x_recv.at[c], xpeer)
 
-    def z_copy(c, d):
-        there = lax.rem(z + d, NZ)
-        return remote(
-            z_out.at[c, there], z_in.at[c, d - 1], z_send.at[c, d - 1], z_recv.at[c, d - 1],
-            zpeer[d - 1],
-        )
-
-    def columns(c, source):
-        return pl.ds(pl.multiple_of(c * WIDE + source * piece, piece), piece)
-
-    def gz_copy(c, d, source):
-        block = out_ref.at[x, :, columns(c, source)]
-        return remote(block, block, gz_send.at[c, d - 1], gz_recv.at[c, d - 1], zpeer[d - 1])
+    def z_copy(c):
+        return remote(z_out.at[c], z_in.at[0, c], z_send.at[c], z_recv.at[c], zpeer)
+
+    def m_copy(c):
+        return remote(z_out.at[c], z_in.at[1, c], m_send.at[c], m_recv.at[c], mpeer)
+
+    def columns(c):
+        return pl.ds(pl.multiple_of(c * WIDE, WIDE), WIDE)
+
+    def g_copy(c):
+        block = out_ref.at[x, :, columns(c)]
+        return remote(block, block, g_send.at[c], g_recv.at[c], zpeer)
 
     def gx_copy(c, side):
-        block = out_ref.at[side, :, pl.ds(pl.multiple_of(c * WIDE, WIDE), WIDE)]
+        block = out_ref.at[side, :, columns(c)]
         return remote(block, block, gx_send.at[c], gx_recv.at[c], xpeer)
 
     def second(c):
@@ -176,27 +178,39 @@
     def join_x(c):
         x_copy(c).wait_recv()
         total = zsum[c] + x_in[c].astype(jnp.float32)
-        zsum[c] = total
-        for k in range(NZ):
-            z_out[c, k] = total[:, k * piece:(k + 1) * piece].astype(jnp.bfloat16)
-        for d in (2, 1, 3):
-            z_copy(c, d).start()
+
+        @pl.when(inner)
+        def _():
+            zsum[c] = total
+
+        @pl.when(jnp.logical_not(inner))
+        def _():
+            z_out[c] = total.astype(jnp.bfloat16)
+            z_copy(c).start()
 
     def join_z(c):
-        total = zsum[c, :, pl.ds(pl.multiple_of(z * piece, piece), piece)]
-        for d in range(1, NZ):
-            z_copy(c, d).wait_recv()
-            total = total + z_in[c, d - 1].astype(jnp.float32)
-        out_ref[x, :, columns(c, z)] = total.astype(jnp.bfloat16)
-        for d in (2, 1, 3):
-            gz_copy(c, d, z).start()
+        @pl.when(inner)
+        def _():
+            z_copy(c).wait_recv()
+            z_out[c] = (zsum[c] + z_in[0, c].astype(jnp.float32)).astype(jnp.bfloat16)
+            m_copy(c).start()
+
+    def join_middle(c):
+        @pl.when(inner)
+        def _():
+            m_copy(c).wait_recv()
+            total = z_out[c].astype(jnp.float32) + z_in[1, c].astype(jnp.float32)
+            out_ref[x, :, columns(c)] = total.astype(jnp.bfloat16)
+            g_copy(c).start()
+            gx_copy(c, x).start()
 
     def pass_x(c):
-        for d in range(1, NZ):
-            gz_copy(c, d, lax.rem(z + NZ - d, NZ)).wait_recv()
-        gx_copy(c, x).start()
-
-    stages = ((0, second), (1, join_cores), (3, join_x), (4, join_z), (5, pass_x))
+        @pl.when(jnp.logical_not(inner))
+        def _():
+            g_copy(c).wait_recv()
+            gx_copy(c, x).start()
+
+    stages = ((0, second), (2, join_cores), (5, join_x), (8, join_z), (11, join_middle), (14, pass_x))
 
     def step(s, carry):
         for lag, stage in stages:
@@ -215,9 +229,16 @@
         gx_copy(c, x).wait_send()
         core_copy(c).wait_send()
         x_copy(c).wait_send()
-        for d in range(1, NZ):
-            z_copy(c, d).wait_send()
-            gz_copy(c, d, z).wait_send()
+
+        @pl.when(inner)
+        def _():
+            m_copy(c).wait_send()
+            g_copy(c).wait_send()
+
+        @pl.when(jnp.logical_not(inner))
+        def _():
+            z_copy(c).wait_send()
+
         return carry
 
     lax.fori_loop(0, chunks, finish, 0)
@@ -251,20 +272,19 @@
             pltpu.VMEM((chunks, half, WIDE), bf16),
             pltpu.VMEM((chunks, half, WIDE), bf16),
             pltpu.VMEM((chunks, half, WIDE), f32),
-            pltpu.VMEM((chunks, NZ, half, WIDE // NZ), bf16),
-            pltpu.VMEM((chunks, NZ - 1, half, WIDE // NZ), bf16),
+            pltpu.VMEM((chunks, half, WIDE), bf16),
+            pltpu.VMEM((2, chunks, half, WIDE), bf16),
             dma((steps, 2)), dma((chunks, 2)), dma((1,)), dma((2,)), dma((2,)),
             dma((chunks,)), dma((chunks,)), dma((chunks,)), dma((chunks,)),
-            dma((chunks, NZ - 1)), dma((chunks, NZ - 1)),
-            dma((chunks, NZ - 1)), dma((chunks, NZ - 1)),
-            dma((chunks,)), dma((chunks,)),
+            dma((chunks,)), dma((chunks,)), dma((chunks,)), dma((chunks,)),
+            dma((chunks,)), dma((chunks,)), dma((chunks,)), dma((chunks,)),
         ],
         compiler_params=pltpu.CompilerParams(
             collective_id=0, has_side_effects=True, vmem_limit_bytes=62 * 1024 * 1024
         ),
         name="fused_experts",
     )(
-        tokens, router_score.reshape(1, rows), expert_ids, gate_up[0], down[0],
+        tokens, router_score.reshape(1, rows), expert_ids.reshape(1, rows), gate_up[0], down[0],
         shared_gate_up, shared_down,
     )
     return out.reshape(rows, width)

time: 63.4 us -> 51.6 us (0.81)
  Pallas kernels: 59.6 us -> 49.3 us
  local copies, waits for them, and re-layouts: 3.58 us -> 2.21 us
    pallas_call x1, Pallas kernels: 59.6 us -> 49.3 us  [fused_device(): pl.pallas_call(fused_kernel, out_shape=jax.ShapeDtypeStruct((NX, half, wi...]
    unnamed x2 -> x1, local copies, waits for them, and re-layouts: 3.58 us -> 2.21 us
where the time goes in v2:
time: 51.6 us; the launch traced here: 51.5 us
  Pallas kernels  49.3 us (96%)
  local copies, waits for them, and re-layouts  2.21 us (4%)
    pallas_call x1, Pallas kernels, fused_device(): pl.pallas_call(fused_kernel, out_shape=jax.ShapeDtypeStruct((NX, half, wi...  49.3 us
    unnamed x1, local copies, waits for them, and re-layouts  2.21 us

profile of v2, /device:TPU:0, one launch (start us, length us, event | category | flops | bytes accessed | tf_op | source)
XLA Modules:
  0.0 51.5 jit_solution(9157067745148500652)
XLA Ops:
  0.0 49.3 %fused_experts.1 = bf16[2,48,5120]{2,1,0:T(8,128)(2,1)} custom-call(bf16[96,5120]{1,0:T(8,128)(2,1)} %tok_ref.1, bf16[1,96]{1,0:T(2,128)(2,1)} %bitcast.8, s32[1,96]{1,0:T(1,128)} %bitcast.9, bf16[5120,2048]{1,0:T(8,128)(2,1)} %bitcast.5, bf16[1024,5120]{1,0:T(8,128)(2,1)} %bitcast.6, bf16[5120,1024]{1,0:T(8,128)(2,1)} %sgu_ref.1, bf16[512,5120]{1,0:T(8,128)(2,1)} %sdown_ref.1), custom_call_target="tpu_custom_call" | custom-call | tf_op jit(solution)/shard_map/fused_experts/pallas_call | solution.py:257
  49.3 2.2 %copy.9 = bf16[96,5120]{1,0:T(8,128)(2,1)} copy(bf16[96,5120]{1,0:T(8,128)(2,1)} %bitcast.7) | data formatting | bytes 1966080

commit v3 on v2

--- a/solution.py
+++ b/solution.py
@@ -280,7 +280,7 @@
             dma((chunks,)), dma((chunks,)), dma((chunks,)), dma((chunks,)),
         ],
         compiler_params=pltpu.CompilerParams(
-            collective_id=0, has_side_effects=True, vmem_limit_bytes=62 * 1024 * 1024
+            collective_id=0, has_side_effects=True, vmem_limit_bytes=52 * 1024 * 1024
         ),
         name="fused_experts",
     )(

time: 51.6 us -> 46.9 us (0.909)
  Pallas kernels: 49.3 us -> 43.2 us
  local copies, waits for them, and re-layouts: 2.21 us -> 3.46 us
    pallas_call x1, Pallas kernels: 49.3 us -> 43.2 us  [fused_device(): pl.pallas_call(fused_kernel, out_shape=jax.ShapeDtypeStruct((NX, half, wi...]
    unnamed x1 -> x7, local copies, waits for them, and re-layouts: 2.21 us -> 3.46 us
where the time goes in v3:
time: 46.9 us; the launch traced here: 46.7 us
  Pallas kernels  43.2 us (92%)
  local copies, waits for them, and re-layouts  3.46 us (7%)
    pallas_call x1, Pallas kernels, fused_device(): pl.pallas_call(fused_kernel, out_shape=jax.ShapeDtypeStruct((NX, half, wi...  43.2 us
    unnamed x7, local copies, waits for them, and re-layouts  3.46 us

profile of v3, /device:TPU:0, one launch (start us, length us, event | category | flops | bytes accessed | tf_op | source)
XLA Modules:
  0.0 46.7 jit_solution(10732116677354202817)
XLA Ops:
  0.0 0.0 copy-start
  0.0 1.2 %copy-done = bf16[96,5120]{1,0:T(8,128)(2,1)S(1)} copy-done((bf16[96,5120]{1,0:T(8,128)(2,1)S(1)}, bf16[96,5120]{1,0:T(8,128)(2,1)}, u32[]{:S(2)}) %copy-start) | copy-done | bytes 983064
  1.2 0.0 copy-start.1
  1.2 0.7 %copy-done.1 = bf16[96]{0:T(256)(128)(2,1)S(1)} copy-done((bf16[96]{0:T(256)(128)(2,1)S(1)}, bf16[96]{0:T(256)(128)(2,1)}, u32[]{:S(2)}) %copy-start.1) | copy-done | bytes 216
  1.9 0.0 copy-start.2
  1.9 0.7 %copy-done.2 = s32[96,1]{0,1:T(1,128)S(1)} copy-done((s32[96,1]{0,1:T(1,128)S(1)}, s32[96,1]{0,1:T(1,128)}, u32[]{:S(2)}) %copy-start.2) | copy-done | bytes 408
  2.5 43.2 %fused_experts.1 = bf16[2,48,5120]{2,1,0:T(8,128)(2,1)S(1)} custom-call(bf16[96,5120]{1,0:T(8,128)(2,1)S(1)} %copy-done, bf16[1,96]{1,0:T(2,128)(2,1)S(1)} %bitcast.6, s32[1,96]{1,0:T(1,128)S(1)} %bitcast.7, bf16[5120,2048]{1,0:T(8,128)(2,1)} %bitcast.8, bf16[1024,5120]{1,0:T(8,128)(2,1)} %bitcast.9, bf16[5120,1024]{1,0:T(8,128)(2,1)} %sgu_ref.1, ...), custom_call_target="tpu_custom_call" | custom-call | tf_op jit(solution)/shard_map/fused_experts/pallas_call | solution.py:257
  45.7 0.9 %copy.9 = bf16[96,5120]{1,0:T(8,128)(2,1)} copy(bf16[96,5120]{1,0:T(8,128)(2,1)S(1)} %bitcast.5) | data formatting | bytes 1966080
Async XLA Ops:
  0.0 1.2 %copy-start = (bf16[96,5120]{1,0:T(8,128)(2,1)S(1)}, bf16[96,5120]{1,0:T(8,128)(2,1)}, u32[]{:S(2)}) copy-start(bf16[96,5120]{1,0:T(8,128)(2,1)} %tok_ref.1) | copy-start | bytes 2949124
  1.2 0.7 %copy-start.1 = (bf16[96]{0:T(256)(128)(2,1)S(1)}, bf16[96]{0:T(256)(128)(2,1)}, u32[]{:S(2)}) copy-start(bf16[96]{0:T(256)(128)(2,1)} %param.8) | copy-start | bytes 580
  1.9 0.7 %copy-start.2 = (s32[96,1]{0,1:T(1,128)S(1)}, s32[96,1]{0,1:T(1,128)}, u32[]{:S(2)}) copy-start(s32[96,1]{0,1:T(1,128)} %param.9) | copy-start | bytes 1156
